TPU v7x, 256 devices: a whole 4x4x8 slice. The times are simulated.
256 devices in a mesh: member: 8 (over x, core), seq: 32 (over z, y).
Axes of the slice: x: 4, y: 4, z: 8, core: 2. Of those that a mesh axis runs over, the one named last changes fastest.
Arguments:
- vertex_embedding_matrix: bfloat16 [8, 16384, 1024], P('member', 'seq'), may hold values from -6 to 6
- norm_gain: float32 [1024], replicated, may hold values from 0.25 to 1.75
- qkv_weight: bfloat16 [1024, 3072], replicated, may hold values from -0.25 to 0.25
- out_weight: bfloat16 [1024, 1024], replicated, may hold values from -0.1875 to 0.1875
- window_reach: int32 [16384], P('seq'), may hold values from 1 to 512, as said below
- decode_weight: bfloat16 [1024, 100], replicated, may hold values from -0.1875 to 0.1875
- cell_nodes: int32 [3, 131072], P(None, 'seq'), may hold values from 0 to 16383, as said below
- cell_coeffs: float32 [3, 131072], P(None, 'seq'), may hold values from 0.2 to 0.6
- targets: bfloat16 [100, 131072], P(None, 'seq'), may hold values from -6 to 6
- area_weight: float32 [131072], P('seq'), as said below
Outputs:
- predicted_maps: bfloat16 [8, 100, 131072], P('member', None, 'seq')
- scoring_penalty: float32 [], replicated
- readout_matrix_derivative: float32 [1024, 100], replicated
Inputs may be any that keep to these rules, and one draw needn't show every extreme that they name: `window_reach`: each node reaches at least one neighbour; the largest reach 512 occurs in every draw. `cell_nodes`: the nodes of cell c lie within 512 positions of c * 512 // 4096. `area_weight`: Positive.
All inputs are finite; a program needn't handle non-finite values.
Results may differ from a plain program's by a relative error of at most 0.009.
Values may be sent and summed in bfloat16 or wider, within the bound.
No kernel may reach another device: no remote copies, remote signals or barrier semaphores. Data moves between devices by JAX's collectives and lax.ppermute only.
A program may use at most 128 MiB of HBM per device.

v0:
```python
import jax
import jax.numpy as jnp
from jax import lax
from jax.sharding import PartitionSpec as P

HEADS = 16
HALF = 512


ALPHA = 0.95
SOFTNESS = 0.01


def padded(cells, sides, width):
    for axis, dim in sides:
        count = lax.axis_size(axis)
        ends = count - 1
        head = lax.slice_in_dim(cells, 0, width, axis=dim)
        tail = lax.slice_in_dim(cells, cells.shape[dim] - width, cells.shape[dim], axis=dim)
        cells = jnp.concatenate(
            [
                lax.ppermute(tail, axis, [(i, (i + 1) % count) for i in range(ends)]),
                cells,
                lax.ppermute(head, axis, [((i + 1) % count, i) for i in range(ends)]),
            ],
            axis=dim,
        )
    return cells


def passed_along(value, axis, by):
    peers = lax.axis_size(axis)
    pairs = [(i, i + by) for i in range(peers) if 0 <= i + by < peers]
    return lax.ppermute(value, axis, pairs)


def soft_size(value):
    return jnp.sqrt(value * value + SOFTNESS)


def slope(value):
    return value / jnp.sqrt(value * value + SOFTNESS)


def window_attention(query, keyval, reach, start, total):
    rows = query.shape[0]
    span = keyval.shape[0]
    width = query.shape[1]
    head_dim = width // HEADS
    groups = max(1, HEADS // 8)
    per_group = HEADS // groups
    group_width = per_group * head_dim
    query_place = start + jnp.arange(rows, dtype=jnp.int32)
    key_place = start - HALF + jnp.arange(span, dtype=jnp.int32)
    inside = (key_place >= 0) & (key_place < total)
    allowed = (jnp.abs(query_place[:, None] - key_place[None, :]) <= reach[:, None]) & inside[
        None, :
    ]

    def one_group(pieces):
        group_query, group_keys, group_values = pieces
        query_heads = group_query.reshape(rows, per_group, head_dim)
        key_heads = group_keys.reshape(span, per_group, head_dim)
        value_heads = group_values.reshape(span, per_group, head_dim)
        scores = jnp.einsum(
            "qhd,khd->hqk", query_heads, key_heads, preferred_element_type=jnp.float32
        ) * head_dim ** (-0.5)
        scores = jnp.where(allowed[None], scores, jnp.float32(-1e30))
        row_max = jnp.max(scores, axis=-1, keepdims=True)
        exponent = jnp.exp(scores - row_max)
        probs = (exponent / jnp.sum(exponent, axis=-1, keepdims=True)).astype(jnp.bfloat16)
        mixed = jnp.einsum("hqk,khd->qhd", probs, value_heads, preferred_element_type=jnp.float32)
        return mixed.astype(jnp.bfloat16).reshape(rows, group_width)

    group_query = query.reshape(rows, groups, group_width).transpose(1, 0, 2)
    group_keys = keyval[:, :width].reshape(span, groups, group_width).transpose(1, 0, 2)
    group_values = keyval[:, width:].reshape(span, groups, group_width).transpose(1, 0, 2)
    mixed = lax.map(one_group, (group_query, group_keys, group_values))
    return mixed.transpose(1, 0, 2).reshape(rows, width)


def grad_terms(own_slope, pair_slopes, weight, count, total_cells):
    fairness = (1.0 - ALPHA) / count
    grad = own_slope / count - (1.0 - fairness) / (count * (count - 1)) * pair_slopes
    return grad * weight / total_cells


def score_sum(sample_predictions_stacked, truth, weight, total_cells):
    count = sample_predictions_stacked.shape[0]
    fairness = (1.0 - ALPHA) / count
    skill = jnp.mean(soft_size(sample_predictions_stacked - truth[None]), axis=0)
    spread = jnp.sum(
        soft_size(sample_predictions_stacked[:, None] - sample_predictions_stacked[None]),
        axis=(0, 1),
    )
    score = skill - (1.0 - fairness) / (2.0 * count * (count - 1)) * spread
    return jnp.sum(weight[None, :] * score) / total_cells


def on_device(
    vertex_embedding_matrix,
    norm_gain,
    qkv_weight,
    out_weight,
    window_reach,
    decode_weight,
    cell_nodes,
    cell_coeffs,
    targets,
    area_weight,
):
    state = vertex_embedding_matrix[0]
    nodes_here = state.shape[0]
    width = state.shape[1]
    cells_here = targets.shape[1]
    seq_count = lax.axis_size("seq")
    segment = lax.axis_index("seq")
    total_nodes = nodes_here * seq_count
    total_cells = cells_here * seq_count
    state_wide = state.astype(jnp.float32)
    normed = (
        state_wide
        * lax.rsqrt(jnp.mean(state_wide * state_wide, axis=-1, keepdims=True) + 1e-05)
        * norm_gain
    ).astype(jnp.bfloat16)
    qkv = jnp.dot(normed, qkv_weight, preferred_element_type=jnp.float32).astype(jnp.bfloat16)
    query = qkv[:, :width]
    keyval = qkv[:, width:]
    keyval_ext = padded(keyval, (("seq", 0),), HALF)
    start = segment * nodes_here
    block = min(nodes_here, 512)

    def one_block(index):
        offset = index * block
        return window_attention(query, keyval_ext, window_reach, start + offset, total_nodes)

    attended = lax.map(one_block, jnp.arange(nodes_here // block, dtype=jnp.int32)).reshape(
        nodes_here, width
    )
    latent = (
        state_wide + jnp.dot(attended, out_weight, preferred_element_type=jnp.float32)
    ).astype(jnp.bfloat16)
    values = jnp.dot(latent, decode_weight, preferred_element_type=jnp.float32).astype(jnp.bfloat16)
    table = padded(values, (("seq", 0),), nodes_here)
    local_index = cell_nodes - (segment - 1) * nodes_here
    picked = table[local_index].astype(jnp.float32)
    lattice_quantities = jnp.sum(cell_coeffs[:, :, None] * picked, axis=0)
    predicted_maps = lattice_quantities.T.astype(jnp.bfloat16)
    member_count = lax.axis_size("member")
    member_place = lax.axis_index("member")
    share = cells_here // member_count
    truth_all = targets.astype(jnp.float32)
    truth_part = lax.dynamic_slice_in_dim(truth_all, member_place * share, share, 1)
    weight_part = lax.dynamic_slice_in_dim(area_weight, member_place * share, share, 0)
    sample_predictions_stacked = lax.all_to_all(
        predicted_maps[None], "member", split_axis=2, concat_axis=0, tiled=True
    ).astype(jnp.float32)
    loss_part = score_sum(sample_predictions_stacked, truth_part, weight_part, total_cells)
    pair_slopes = jnp.sum(
        slope(sample_predictions_stacked[:, None] - sample_predictions_stacked[None]), axis=1
    )
    grads = grad_terms(
        slope(sample_predictions_stacked - truth_part[None]),
        pair_slopes,
        weight_part,
        member_count,
        total_cells,
    )
    cell_grad = lax.all_to_all(
        grads.astype(jnp.bfloat16), "member", split_axis=0, concat_axis=2, tiled=True
    ).astype(grads.dtype)[0]
    terms = cell_coeffs[:, :, None] * cell_grad.T[None, :, :]
    spread_index = (cell_nodes - (segment - 1) * nodes_here).reshape(-1)
    collected = jax.ops.segment_sum(
        terms.reshape(-1, terms.shape[2]), spread_index, num_segments=3 * nodes_here
    )
    lower = collected[:nodes_here]
    middle = collected[nodes_here : 2 * nodes_here]
    upper = collected[2 * nodes_here :]
    from_next = passed_along(lower.astype(jnp.bfloat16), "seq", -1).astype(lower.dtype)
    from_prev = passed_along(upper.astype(jnp.bfloat16), "seq", 1).astype(upper.dtype)
    node_grad = (middle + from_next + from_prev).astype(jnp.bfloat16)
    partial_grad = lax.dot_general(
        latent, node_grad, (((0,), (0,)), ((), ())), preferred_element_type=jnp.float32
    )
    readout_matrix_derivative, scoring_penalty = lax.psum(
        (partial_grad, loss_part), ("member", "seq")
    )
    return (predicted_maps[None], scoring_penalty, readout_matrix_derivative)


def solution(mesh):
    placed = (
        P("member", "seq", None),
        P(),
        P(),
        P(),
        P("seq"),
        P(),
        P(None, "seq"),
        P(None, "seq"),
        P(None, "seq"),
        P("seq"),
    )
    return jax.shard_map(
        on_device,
        mesh=mesh,
        in_specs=placed,
        out_specs=(P("member", None, "seq"), P(), P()),
        check_vma=False,
    )
```

profile of v0, /device:TPU:2, one launch (start us, length us, event | category | flops | bytes accessed | tf_op | source)
XLA Modules:
  0.0 695.0 jit_solution(8100286381026976864)
XLA Ops:
  8.8 6.6 convolution_convert_fusion
  20.1 5.9 collective-permute-start
  28.7 39.7 %collective-permute-done.1 = bf16[512,2048]{1,0:T(8,128)(2,1)} collective-permute-done((bf16[512,2048]{1,0:T(8,128)(2,1)}, bf16[512,2048]{1,0:T(8,128)(2,1)}, u32[]{:S(2)}, u32[]{:S(2)}) %collective-permute-start.1) | collective-permute-done | bytes 2097184 | tf_op jit(solution)/shard_map/ppermute | solution.py:24
  86.3 57.3 %while.18 = (s32[]{:T(128)}, bf16[2,512,512]{1,2,0:T(8,128)(2,1)}, bf16[2,1536,512]{1,2,0:T(8,128)(2,1)}, bf16[2,512,512]{1,2,0:T(8,128)(2,1)}, bf16[2,1536,512]...) while((s32[]{:T(128)}, bf16[2,512,512]{1,2,0:T(8,128)(2,1)}, ...), condition=%wide.region_4.5_spmd.clone, body=%wide.region_1.4_spmd.clone.sunk | while | flops 2475957248 | bytes 19181204 | solution.py:78
  92.4 9.5 %fusion.68 = f32[8,512]{1,0:T(8,128)S(1)} fusion(pred[512,1536]{1,0:T(8,128)(4,1)S(1)} %fusion.67, bf16[512,8,64]{0,2,1:T(8,128)(2,1)S(1)} %bitcast.112, bf16[1536,8,64]{0,2,1:T(8,128)(2,1)} %bitcast.104), kind=kOutput, calls=%fused_computation.73.clone.1 | convolution fusion | flops 830473728 | bytes 2899968 | tf_op jit(solution)/shard_map/while/body/eval_jaxpr/while/body/eval_jaxpr/sub | solution.py:70
  101.9 12.1 %fusion.69 = bf16[8,64,512]{2,1,0:T(8,128)(2,1)S(1)} fusion(bf16[1536,8,64]{0,2,1:T(8,128)(2,1)} %bitcast.106, f32[8,512]{1,0:T(8,128)S(1)} %fusion.68, pred[512,1536]{1,0:T(8,128)(4,1)S(1)} %fusion.67, bf16[512,8,64]{0,2,1:T(8,128)(2,1)} %bitcast.113, bf16[1536,8,64]{0,2,1:T(8,128)(2,1)} %bitcast.105), kind=kOutput, calls=%fused_computation.14.clone.1 | convolution fusion | flops 1642337792 | bytes 4997120 | tf_op jit(solution)/shard_map/while/body/eval_jaxpr/while/body/eval_jaxpr/hqk,khd->qhd/dot_general | solution.py:72
  120.8 9.5 %fusion.68 = f32[8,512]{1,0:T(8,128)S(1)} fusion(pred[512,1536]{1,0:T(8,128)(4,1)S(1)} %fusion.67, bf16[512,8,64]{0,2,1:T(8,128)(2,1)S(1)} %bitcast.112, bf16[1536,8,64]{0,2,1:T(8,128)(2,1)} %bitcast.104), kind=kOutput, calls=%fused_computation.73.clone.1 | convolution fusion | flops 830473728 | bytes 2899968 | tf_op jit(solution)/shard_map/while/body/eval_jaxpr/while/body/eval_jaxpr/sub | solution.py:70
  130.3 12.1 %fusion.69 = bf16[8,64,512]{2,1,0:T(8,128)(2,1)S(1)} fusion(bf16[1536,8,64]{0,2,1:T(8,128)(2,1)} %bitcast.106, f32[8,512]{1,0:T(8,128)S(1)} %fusion.68, pred[512,1536]{1,0:T(8,128)(4,1)S(1)} %fusion.67, bf16[512,8,64]{0,2,1:T(8,128)(2,1)} %bitcast.113, bf16[1536,8,64]{0,2,1:T(8,128)(2,1)} %bitcast.105), kind=kOutput, calls=%fused_computation.14.clone.1 | convolution fusion | flops 1642337792 | bytes 4997120 | tf_op jit(solution)/shard_map/while/body/eval_jaxpr/while/body/eval_jaxpr/hqk,khd->qhd/dot_general | solution.py:72
  148.3 5.0 collective-permute-start.2
  155.9 43.3 %gather_fusion = bf16[12288,100]{1,0:T(8,128)(2,1)} fusion(bf16[1536,100]{1,0:T(8,128)(2,1)S(1)} %copy.58, s32[12288]{0:T(1024)S(1)} %broadcast_clamp_fusion), kind=kCustom, calls=%fused_computation | custom fusion | bytes 4964352 | tf_op jit(solution)/shard_map/gather | solution.py:146
  204.3 17.0 %copy.82 = bf16[1,100,4096]{1,0,2:T(2,128)(2,1)} copy(bf16[1,100,4096]{1,2,0:T(8,128)(2,1)S(1)} %bitcast.116) | data formatting | bytes 1638400 | tf_op jit(solution)/shard_map/broadcast_in_dim | solution.py:189
  221.8 23.6 %reduce = bf16[4096,100]{1,0:T(8,128)(2,1)S(1)} reduce(bf16[4096,1,100]{2,1,0:T(2,128)(2,1)} %bitcast.118, bf16[]{:T(256)} %broadcast.93), dimensions={1}, to_apply=%bitcast.85.reduce_sub_computation | reduce | bytes 1638402
  249.9 4.8 all-to-all-start
  256.4 10.4 %all-to-all-done = bf16[8,2,25600]{2,1,0:T(2,128)(2,1)S(1)} async-done(((bf16[8,2,25600]{2,1,0:T(2,128)(2,1)}), bf16[8,2,25600]{2,1,0:T(2,128)(2,1)S(1)}, u32[]{:S(2)}, u32[]{:S(2)}) %all-to-all-start) | async-done | bytes 819232 | tf_op jit(solution)/shard_map/all_to_all | solution.py:155
  266.8 5.6 reshape.129
  272.3 4.8 copy.60
  280.0 24.2 %fusion.22 = (f32[8,100,512]{2,1,0:T(8,128)S(1)}, f32[100,512]{1,0:T(8,128)}) fusion(f32[8,100,512]{2,0,1:T(8,128)S(1)} %get-tuple-element.122, f32[8,100,512]{2,1,0:T(8,128)S(1)} %bitcast.125), kind=kLoop, calls=%fused_computation.30 | loop fusion | flops 19200000 | bytes 5120000 | tf_op jit(solution)/shard_map/reduce_sum | solution.py:159
  306.8 4.9 all-to-all-start.1
  311.8 12.3 %all-to-all-done.1 = bf16[8,100,512]{2,1,0:T(8,128)(2,1)S(1)} async-done(((bf16[8,100,512]{2,1,0:T(8,128)(2,1)}), bf16[8,100,512]{2,1,0:T(8,128)(2,1)S(1)}, u32[]{:S(2)}, u32[]{:S(2)}) %all-to-all-start.1) | async-done | bytes 819232 | tf_op jit(solution)/shard_map/all_to_all | solution.py:169
  337.9 6.6 copy.64
  344.5 66.9 %scatter_custom_fusion = f32[1536,100]{1,0:T(8,128)} fusion(s32[12288]{0:T(1024)S(1)} %reshape.113, f32[12288,100]{1,0:T(8,128)} %copy.64, f32[]{:T(128)} %constant.29.clone.1), kind=kCustom, calls=%fused_computation.56 | custom fusion | flops 1228800 | bytes 614912 | tf_op jit(solution)/shard_map/scatter-add | solution.py:174
  413.9 4.9 collective-permute-start.5
  427.5 88.6 %psum.14 = f32[]{:T(128)} all-reduce(f32[]{:T(128)S(6)} %div.45), channel_id=1, replica_groups=mesh['member'=8,'seq'=32] {'member','seq'}, use_global_device_ids=true, to_apply=%region_9.10 | all-reduce | flops 1 | bytes 8 | tf_op jit(solution)/shard_map/psum | solution.py:186
  516.1 170.0 %all-reduce.2.cloned.1.call-done = f32[1024,100]{0,1:T(8,128)} async-done(((f32[1024,100]{0,1:T(8,128)}), f32[1024,100]{0,1:T(8,128)}) %all-reduce.2.cloned.1.call-update) | async-done | bytes 409616 | tf_op jit(solution)/shard_map/psum | solution.py:186
  (91 shorter events, 90.5 us)
Async XLA Ops:
  7.2 136.5 %copy-start = (bf16[1024,1024]{1,0:T(8,128)(2,1)S(1)}, bf16[1024,1024]{1,0:T(8,128)(2,1)}, u32[]{:S(2)}) copy-start(bf16[1024,1024]{1,0:T(8,128)(2,1)} %param.15) | copy-start | bytes 6291460
  15.5 1.7 copy-start.5
  17.2 8.9 %copy-start.10 = (s32[3,4096]{1,0:T(4,128)S(1)}, s32[3,4096]{1,0:T(4,128)}, u32[]{:S(2)}) copy-start(s32[3,4096]{1,0:T(4,128)} %param.18) | copy-start | bytes 147460
  18.7 8.7 %slice-start = ((bf16[512,3072]{1,0:T(8,128)(2,1)}), bf16[512,1024]{1,0:T(8,128)(2,1)S(1)}, s32[]{:S(2)}) async-start(bf16[512,3072]{1,0:T(8,128)(2,1)} %copy-done.5), calls=%async_computation.3 | async-start | bytes 2097152 | tf_op jit(solution)/shard_map/slice | solution.py:127
  18.7 49.7 %collective-permute-start.1 = (bf16[512,2048]{1,0:T(8,128)(2,1)}, bf16[512,2048]{1,0:T(8,128)(2,1)}, u32[]{:S(2)}, u32[]{:S(2)}) collective-permute-start(bf16[512,2048]{1,0:T(8,128)(2,1)} %slice.34), channel_id=1, source_target_pairs={{1,0},{2,1},{3,2},{4,3},{5,4},{6,5},{7,6},{8,7},{9,8},{10,9},{11,1... | collective-permute-start | bytes 6291464 | tf_op jit(solution)/shard_map/ppermute | solution.py:24
  20.1 49.5 %collective-permute-start = (bf16[512,2048]{1,0:T(8,128)(2,1)}, bf16[512,2048]{1,0:T(8,128)(2,1)}, u32[]{:S(2)}, u32[]{:S(2)}) collective-permute-start(bf16[512,2048]{1,0:T(8,128)(2,1)} %slice.34), channel_id=1, source_target_pairs={{0,1},{1,2},{2,3},{3,4},{4,5},{5,6},{6,7},{7,8},{8,9},{9,10},{10,1... | collective-permute-start | bytes 6291464 | tf_op jit(solution)/shard_map/ppermute | solution.py:22
  81.6 4.7 copy-start.11
  87.6 4.8 copy-start.1
  116.0 4.8 copy-start.1
  143.7 2.9 copy-start.8
  143.7 9.7 %copy-start.9 = (s32[12288]{0:T(1024)S(1)}, s32[12288]{0:T(1024)}, u32[]{:S(2)}) copy-start(s32[12288]{0:T(1024)} %reshape.105) | copy-start | bytes 147460
  146.5 9.1 %copy-start.4 = (bf16[512,1024]{1,0:T(8,128)(2,1)}, bf16[512,1024]{1,0:T(8,128)(2,1)S(1)}, u32[]{:S(2)}) copy-start(bf16[512,1024]{1,0:T(8,128)(2,1)S(1)} %fusion.27) | copy-start | bytes 3145732
  147.0 7.1 %collective-permute-start.3 = (bf16[512,100]{0,1:T(8,128)(2,1)S(1)}, bf16[512,100]{0,1:T(8,128)(2,1)S(1)}, u32[]{:S(2)}, u32[]{:S(2)}) collective-permute-start(bf16[512,100]{0,1:T(8,128)(2,1)S(1)} %convolution_convert_fusion.1), channel_id=1, source_target_pairs={{1,0},{2,1},{3,2},{4,3},{5,4},{6,5},{7,6},{8,7},{9,8},{10,9},{11,1... | collective-permute-start | bytes 307208 | tf_op jit(solution)/shard_map/ppermute | solution.py:24
  148.3 7.3 %collective-permute-start.2 = (bf16[512,100]{0,1:T(8,128)(2,1)S(1)}, bf16[512,100]{0,1:T(8,128)(2,1)S(1)}, u32[]{:S(2)}, u32[]{:S(2)}) collective-permute-start(bf16[512,100]{0,1:T(8,128)(2,1)S(1)} %convolution_convert_fusion.1), channel_id=1, source_target_pairs={{0,1},{1,2},{2,3},{3,4},{4,5},{5,6},{6,7},{7,8},{8,9},{9,10},{10,1... | collective-permute-start | bytes 307208 | tf_op jit(solution)/shard_map/ppermute | solution.py:22
  155.9 43.3 %copy-start.6 = (f32[3,4096]{1,0:T(4,128)S(1)}, f32[3,4096]{1,0:T(4,128)}, u32[]{:S(2)}) copy-start(f32[3,4096]{1,0:T(4,128)} %param.19) | copy-start | bytes 147460
  203.2 1.0 copy-start.2
  249.9 16.9 %all-to-all-start = ((bf16[8,2,25600]{2,1,0:T(2,128)(2,1)}), bf16[8,2,25600]{2,1,0:T(2,128)(2,1)S(1)}, u32[]{:S(2)}, u32[]{:S(2)}) async-start(bf16[8,2,25600]{2,1,0:T(2,128)(2,1)} %reshape.128), calls=%async_computation | async-start | bytes 1638400 | tf_op jit(solution)/shard_map/all_to_all | solution.py:155
  304.2 7.5 %copy-start.7 = (s32[3,4096]{1,0:T(4,128)S(1)}, s32[3,4096]{1,0:T(4,128)}, u32[]{:S(2)}) copy-start(s32[3,4096]{1,0:T(4,128)} %get-tuple-element.114) | copy-start | bytes 147460
  306.8 17.3 %all-to-all-start.1 = ((bf16[8,100,512]{2,1,0:T(8,128)(2,1)}), bf16[8,100,512]{2,1,0:T(8,128)(2,1)S(1)}, u32[]{:S(2)}, u32[]{:S(2)}) async-start(bf16[8,100,512]{2,1,0:T(8,128)(2,1)} %get-tuple-element.119), calls=%async_computation.1 | async-start | bytes 1703936 | tf_op jit(solution)/shard_map/all_to_all | solution.py:169
  311.7 374.4 %all-reduce.2.cloned.1.call-start = ((), (), s32[]{:S(2)}) async-start(), calls=%async_computation.2 | async-start | bytes 851968 | tf_op jit(solution)/shard_map/psum | solution.py:186
  344.5 81.6 %copy-start.3 = (bf16[4096,100]{1,0:T(8,128)(2,1)S(1)}, bf16[4096,100]{1,0:T(8,128)(2,1)}, u32[]{:S(2)}) copy-start(bf16[4096,100]{1,0:T(8,128)(2,1)} %copy-done.2) | copy-start | bytes 2457604
  412.6 7.6 %collective-permute-start.4 = (bf16[512,100]{1,0:T(8,128)(2,1)S(1)}, bf16[512,100]{1,0:T(8,128)(2,1)S(1)}, u32[]{:S(2)}, u32[]{:S(2)}) collective-permute-start(bf16[512,100]{1,0:T(8,128)(2,1)S(1)} %get-tuple-element.123), channel_id=1, source_target_pairs={{1,0},{2,1},{3,2},{4,3},{5,4},{6,5},{7,6},{8,7},{9,8},{10,9},{11,1... | collective-permute-start | bytes 307208 | tf_op jit(solution)/shard_map/ppermute | solution.py:34
  413.9 7.5 %collective-permute-start.5 = (bf16[512,100]{1,0:T(8,128)(2,1)S(1)}, bf16[512,100]{1,0:T(8,128)(2,1)S(1)}, u32[]{:S(2)}, u32[]{:S(2)}) collective-permute-start(bf16[512,100]{1,0:T(8,128)(2,1)S(1)} %get-tuple-element.124), channel_id=1, source_target_pairs={{0,1},{1,2},{2,3},{3,4},{4,5},{5,6},{6,7},{7,8},{8,9},{9,10},{10,1... | collective-permute-start | bytes 307208 | tf_op jit(solution)/shard_map/ppermute | solution.py:34
Sparse Core Ops, SparseCore 0:
  424.0 262.0 all-reduce.1
where the time goes:
time: 700 us; the launch traced here: 695 us
  waiting for transfers between devices  238 us (34%)
  other arithmetic  137 us (20%)
  local copies, waits for them, and re-layouts  130 us (19%)
  blocking collectives  88.6 us (13%)
  matrix products  55.5 us (8%)
  starting transfers between devices  29.7 us (4%)
  between operations  15.3 us (2%)
    psum x1, waiting for transfers between devices, on_device(): lax.psum((partial_grad, loss_part), ('member', 'seq'))  170 us
    psum x1, blocking collectives, on_device(): lax.psum((partial_grad, loss_part), ('member', 'seq'))  88.6 us
    scatter-add x1, other arithmetic, on_device(): jax.ops.segment_sum(terms.reshape(-1, terms.shape[2]), spread_index, num_...  66.9 us
    gather x1, local copies, waits for them, and re-layouts, on_device(): picked = table[local_index].astype(jnp.float32)  43.3 us
    ppermute x2, waiting for transfers between devices, padded(): lax.ppermute(head, axis, [((i + 1) % count, i) for i in range(ends)])  40.4 us
    unnamed x33, local copies, waits for them, and re-layouts  27.3 us
    reduce_sum x1, other arithmetic, on_device(): jnp.sum(slope(sample_predictions_stacked[:, None] - sample_predictions_st...  24.2 us
    dot_general x2, matrix products, one_group(): jnp.einsum('hqk,khd->qhd', probs, value_heads, preferred_element_type=jnp...  24.2 us
  transfers between devices with their start and end apart: 9, of which 9 were waited for; matrix products, arithmetic and copies ran while one was open for 1% of the time, Pallas kernels for 0%

commit v1 on v0

v1 whole, which is shorter than its diff:
```python
import functools

import jax
import jax.numpy as jnp
from jax import lax
from jax.experimental import pallas as pl
from jax.experimental.pallas import tpu as pltpu
from jax.sharding import PartitionSpec as P

HEADS = 16
HALF = 512
ALPHA = 0.95
SOFTNESS = 0.01
MASKED = -1e30
LOG2E = 1.4426950408889634
STEPS = 4
BLOCKS = 4
F32 = jnp.float32
BF16 = jnp.bfloat16


def params(mib):
    return pltpu.CompilerParams(
        dimension_semantics=("arbitrary",), vmem_limit_bytes=mib * 1024 * 1024
    )


def rows_by_rows(left, right):
    return lax.dot_general(left, right, (((1,), (1,)), ((), ())), preferred_element_type=F32)


def matmul(left, right):
    return jnp.dot(left, right, preferred_element_type=F32)


def layer_norm(state, gain):
    wide = state.astype(F32)
    size = jnp.mean(wide * wide, axis=-1, keepdims=True)
    return (wide * lax.rsqrt(size + 1e-05) * gain).astype(BF16)


def one_head_rows(query, head):
    blank = jnp.zeros_like(query)
    return jnp.concatenate([query, blank] if head % 2 == 0 else [blank, query], axis=0)


def own_kernel(
    state_ref, gain_ref, reach_ref, wq_ref, wk_ref, wv_ref, q_ref, acc_ref, ml_ref, normed, bias
):
    nodes = state_ref.shape[0]
    half = nodes // 2

    @pl.when(pl.program_id(0) == 0)
    def _():
        normed[...] = layer_norm(state_ref[...], gain_ref[...])
        key = lax.broadcasted_iota(jnp.int32, (nodes, nodes), 0)
        place = lax.broadcasted_iota(jnp.int32, (nodes, nodes), 1)
        bias[...] = jnp.where(jnp.abs(place - key) <= reach_ref[...], 0.0, MASKED)

    width = wk_ref.shape[1]
    head_dim = 64
    rows = normed[...]
    query = (rows_by_rows(wq_ref[...], rows) * (LOG2E * head_dim**-0.5)).astype(BF16)
    q_ref[...] = query
    key = matmul(rows, wk_ref[...]).astype(BF16)
    value = rows_by_rows(wv_ref[...], rows).astype(BF16)
    for head in range(width // head_dim):
        span = slice(head * head_dim, (head + 1) * head_dim)
        pair = slice(head // 2 * 128, head // 2 * 128 + 128)
        padded_query = one_head_rows(query[span], head)
        for part in range(2):
            cols = slice(part * half, (part + 1) * half)
            scores = matmul(key[:, pair], padded_query[:, cols]) + bias[:, cols]
            top = jnp.max(scores, axis=0, keepdims=True)
            probs = jnp.exp2(scores - top)
            ml_ref[0, head : head + 1, cols] = top
            ml_ref[0, 4 + head : 5 + head, cols] = jnp.sum(probs, axis=0, keepdims=True)
            acc_ref[span, cols] = matmul(value[span], probs.astype(BF16))


def halo_kernel(
    place_ref,
    prev_ref,
    next_ref,
    state_ref,
    gain_ref,
    reach_ref,
    q_ref,
    acc_ref,
    ml_ref,
    wk_ref,
    wv_ref,
    wo_ref,
    decode_ref,
    latent_ref,
    values_ref,
    normed,
    bias,
    total,
):
    nodes = state_ref.shape[0]
    half = nodes // 2
    step = pl.program_id(0)

    @pl.when(step == 0)
    def _():
        normed[:nodes] = layer_norm(prev_ref[...], gain_ref[...])
        normed[nodes:] = layer_norm(next_ref[...], gain_ref[...])
        total[...] = jnp.zeros_like(total)
        has_prev = place_ref[0] > 0
        has_next = place_ref[0] < place_ref[1] - 1
        for part in range(2):
            key = lax.broadcasted_iota(jnp.int32, (3 * half, half), 0) + part * half
            place = lax.broadcasted_iota(jnp.int32, (3 * half, half), 1) + part * half
            before = key < nodes
            gap = jnp.where(before, place + nodes - key, key - place)
            there = (before & has_prev) | (~before & has_next)
            reach = reach_ref[:, part * half : (part + 1) * half]
            bias[part] = jnp.where((gap <= reach) & there, 0.0, MASKED)

    width = wk_ref.shape[1]
    head_dim = 64
    rows = normed[...]
    key = matmul(rows, wk_ref[...]).astype(BF16)
    value = rows_by_rows(wv_ref[...], rows).astype(BF16)
    query = q_ref[...]
    outs = []
    for head in range(width // head_dim):
        span = slice(head * head_dim, (head + 1) * head_dim)
        pair = slice(head // 2 * 128, head // 2 * 128 + 128)
        padded_query = one_head_rows(query[span], head)
        pieces = []
        for part in range(2):
            cols = slice(part * half, (part + 1) * half)
            near = slice(part * half, (part + 3) * half)
            scores = matmul(key[near, pair], padded_query[:, cols]) + bias[part]
            old_top = ml_ref[0, head : head + 1, cols]
            top = jnp.maximum(old_top, jnp.max(scores, axis=0, keepdims=True))
            probs = jnp.exp2(scores - top)
            shrink = jnp.exp2(old_top - top)
            size = ml_ref[0, 4 + head : 5 + head, cols] * shrink + jnp.sum(
                probs, axis=0, keepdims=True
            )
            mixed = acc_ref[span, cols] * shrink + matmul(value[span, near], probs.astype(BF16))
            pieces.append((mixed / size).astype(BF16))
        outs.append(jnp.concatenate(pieces, axis=1))
    attended = jnp.concatenate(outs, axis=0)
    total[...] += lax.dot_general(
        attended, wo_ref[...], (((0,), (0,)), ((), ())), preferred_element_type=F32
    )

    @pl.when(step == pl.num_programs(0) - 1)
    def _():
        latent = (state_ref[...].astype(F32) + total[...]).astype(BF16)
        latent_ref[...] = latent
        values_ref[...] = rows_by_rows(decode_ref[...], latent).astype(BF16)


def weave_kernel(index_ref, coeff_ref, out_ref):
    window, cells = out_ref.shape[1:]
    chunk = 128

    def rows(at, _):
        first = pl.multiple_of(at * chunk, chunk)
        row = lax.broadcasted_iota(jnp.int32, (chunk, cells), 0) + first
        total = jnp.zeros((chunk, cells), F32)
        for k in range(index_ref.shape[0]):
            total += jnp.where(index_ref[k : k + 1, :] == row, coeff_ref[k : k + 1, :], 0.0)
        out_ref[0, pl.ds(first, chunk), :] = total.astype(BF16)
        return 0

    lax.fori_loop(0, window // chunk, rows, 0)


def decode_kernel(prev_ref, own_ref, next_ref, weave_ref, maps_ref, send_ref, table):
    step = pl.program_id(0)
    nodes = own_ref.shape[1]

    @pl.when(step == 0)
    def _():
        table[:, :nodes] = prev_ref[...]
        table[:, nodes : 2 * nodes] = own_ref[...]
        table[:, 2 * nodes :] = next_ref[...]

    window = weave_ref.shape[1]
    first = pl.multiple_of(step * 128, 128)
    maps = matmul(table[:, pl.ds(first, window)], weave_ref[0]).astype(BF16)
    maps_ref[0] = maps
    share = send_ref.shape[2]
    for part in range(send_ref.shape[0]):
        send_ref[part] = maps[:, part * share : (part + 1) * share]


def score_kernel(members_total, cells_total, maps_ref, truth_ref, weight_ref, grad_ref, loss_ref):
    count = members_total
    fairness = (1.0 - ALPHA) / count
    own_share = 1.0 / count
    pair_share = (1.0 - fairness) / (count * (count - 1))
    rows_total, width = truth_ref.shape
    weight = weight_ref[...] / cells_total
    loss = jnp.zeros((1, width), F32)
    for first in range(0, rows_total, 16):
        rows = slice(first, min(first + 16, rows_total))
        maps = [maps_ref[m, rows, :].astype(F32) for m in range(count)]
        truth = truth_ref[rows, :].astype(F32)
        skill = None
        grads = []
        for m in range(count):
            gap = maps[m] - truth
            square = gap * gap + SOFTNESS
            inverse = lax.rsqrt(square)
            size = square * inverse
            skill = size if skill is None else skill + size
            grads.append(gap * inverse * own_share)
        spread = None
        slopes = [None] * count
        for m in range(count):
            for other in range(m + 1, count):
                gap = maps[m] - maps[other]
                square = gap * gap + SOFTNESS
                inverse = lax.rsqrt(square)
                size = square * inverse
                spread = size if spread is None else spread + size
                slope = gap * inverse
                slopes[m] = slope if slopes[m] is None else slopes[m] + slope
                slopes[other] = -slope if slopes[other] is None else slopes[other] - slope
        for m in range(count):
            grad_ref[m, rows, :] = ((grads[m] - pair_share * slopes[m]) * weight).astype(BF16)
        spread_total = 2.0 * spread + count * SOFTNESS**0.5
        score = skill * own_share - (0.5 * pair_share) * spread_total
        loss += jnp.sum(score, axis=0, keepdims=True)
    loss_ref[...] = loss * weight


def gradient_kernel(
    grad_ref, weave_ref, prev_ref, own_ref, next_ref, loss_ref, out_ref, node_grad
):
    step = pl.program_id(0)

    @pl.when(step == 0)
    def _():
        node_grad[...] = jnp.zeros_like(node_grad)

    window = weave_ref.shape[1]
    first = pl.multiple_of(step * 128, 128)
    grad = jnp.concatenate([grad_ref[part] for part in range(grad_ref.shape[0])], axis=1)
    node_grad[:, pl.ds(first, window)] += rows_by_rows(grad, weave_ref[0])

    @pl.when(step == pl.num_programs(0) - 1)
    def _():
        nodes = own_ref.shape[0]
        terms = node_grad[...].astype(BF16)
        total = matmul(terms[:, :nodes], prev_ref[...])
        total += matmul(terms[:, nodes : 2 * nodes], own_ref[...])
        total += matmul(terms[:, 2 * nodes :], next_ref[...])
        rows = total.shape[0]
        loss = jnp.sum(loss_ref[...], axis=1, keepdims=True)
        chunk = out_ref.shape[2]
        for part in range(out_ref.shape[0]):
            out_ref[part, :rows, :] = total[:, part * chunk : (part + 1) * chunk]
            out_ref[part, rows:, :] = jnp.broadcast_to(loss, (out_ref.shape[1] - rows, chunk))


def whole(*shape):
    return pl.BlockSpec(shape, lambda i: (0,) * len(shape))


def summed_over(value, axis):
    return jnp.sum(lax.all_to_all(value, axis, split_axis=0, concat_axis=0, tiled=True), axis=0)


def gathered_over(value, axis):
    copies = jnp.broadcast_to(value[None], (lax.axis_size(axis),) + value.shape)
    return lax.all_to_all(copies, axis, split_axis=0, concat_axis=0, tiled=True)


def on_device(
    vertex_embedding_matrix,
    norm_gain,
    qkv_weight,
    out_weight,
    window_reach,
    decode_weight,
    cell_nodes,
    cell_coeffs,
    targets,
    area_weight,
):
    state = vertex_embedding_matrix[0]
    nodes, width = state.shape
    variables, cells = targets.shape
    seq_count = lax.axis_size("seq")
    members = lax.axis_size("member")
    segment = lax.axis_index("seq")
    total_cells = cells * seq_count
    share = cells // members
    onward = [(i, (i + 1) % seq_count) for i in range(seq_count)]
    back = [((i + 1) % seq_count, i) for i in range(seq_count)]

    prev_state = lax.ppermute(state, "seq", onward)
    next_state = lax.ppermute(state, "seq", back)

    gain = norm_gain[None, :]
    reach = window_reach[None, :]
    query_weight = qkv_weight[:, :width].T
    value_weight = qkv_weight[:, 2 * width :].T
    group = width // STEPS
    heads = HEADS // STEPS
    query, partial, sizes = pl.pallas_call(
        own_kernel,
        grid=(STEPS,),
        in_specs=[
            whole(nodes, width),
            whole(1, width),
            whole(1, nodes),
            pl.BlockSpec((group, width), lambda i: (i, 0)),
            pl.BlockSpec((width, group), lambda i: (0, STEPS + i)),
            pl.BlockSpec((group, width), lambda i: (i, 0)),
        ],
        out_specs=[
            pl.BlockSpec((group, nodes), lambda i: (i, 0)),
            pl.BlockSpec((group, nodes), lambda i: (i, 0)),
            pl.BlockSpec((1, 2 * heads, nodes), lambda i: (i, 0, 0)),
        ],
        out_shape=[
            jax.ShapeDtypeStruct((width, nodes), BF16),
            jax.ShapeDtypeStruct((width, nodes), F32),
            jax.ShapeDtypeStruct((STEPS, 2 * heads, nodes), F32),
        ],
        scratch_shapes=[pltpu.VMEM((nodes, width), BF16), pltpu.VMEM((nodes, nodes), F32)],
        compiler_params=params(40),
        cost_estimate=pl.CostEstimate(
            flops=20 * 10**9, bytes_accessed=12 * 10**6, transcendentals=4 * 10**6
        ),
        name="own_window",
    )(state, gain, reach, query_weight, qkv_weight, value_weight)

    block = cells // BLOCKS
    block_nodes = nodes // BLOCKS
    window = 2 * nodes + block_nodes
    first = (segment - 1) * nodes + jnp.arange(cells, dtype=jnp.int32) // block * block_nodes
    weave = pl.pallas_call(
        weave_kernel,
        grid=(BLOCKS,),
        in_specs=[
            pl.BlockSpec((3, block), lambda i: (0, i)),
            pl.BlockSpec((3, block), lambda i: (0, i)),
        ],
        out_specs=pl.BlockSpec((1, window, block), lambda i: (i, 0, 0)),
        out_shape=jax.ShapeDtypeStruct((BLOCKS, window, block), BF16),
        compiler_params=params(24),
        cost_estimate=pl.CostEstimate(
            flops=10**9, bytes_accessed=10 * 10**6, transcendentals=0
        ),
        name="weave",
    )(cell_nodes - first[None, :], cell_coeffs)

    place = jnp.stack([segment, jnp.int32(seq_count)])
    latent, values = pl.pallas_call(
        halo_kernel,
        grid=(STEPS,),
        in_specs=[
            pl.BlockSpec(memory_space=pltpu.SMEM),
            whole(nodes, width),
            whole(nodes, width),
            whole(nodes, width),
            whole(1, width),
            whole(1, nodes),
            pl.BlockSpec((group, nodes), lambda i: (i, 0)),
            pl.BlockSpec((group, nodes), lambda i: (i, 0)),
            pl.BlockSpec((1, 2 * heads, nodes), lambda i: (i, 0, 0)),
            pl.BlockSpec((width, group), lambda i: (0, STEPS + i)),
            pl.BlockSpec((group, width), lambda i: (i, 0)),
            pl.BlockSpec((group, width), lambda i: (i, 0)),
            whole(variables, width),
        ],
        out_specs=[whole(nodes, width), whole(variables, nodes)],
        out_shape=[
            jax.ShapeDtypeStruct((nodes, width), BF16),
            jax.ShapeDtypeStruct((variables, nodes), BF16),
        ],
        scratch_shapes=[
            pltpu.VMEM((2 * nodes, width), BF16),
            pltpu.VMEM((2, 3 * nodes // 2, nodes // 2), F32),
            pltpu.VMEM((nodes, width), F32),
        ],
        compiler_params=params(48),
        cost_estimate=pl.CostEstimate(
            flops=30 * 10**9, bytes_accessed=16 * 10**6, transcendentals=6 * 10**6
        ),
        name="halo_window",
    )(
        place,
        prev_state,
        next_state,
        state,
        gain,
        reach,
        query,
        partial,
        sizes,
        qkv_weight,
        value_weight,
        out_weight,
        decode_weight.T,
    )

    prev_values = lax.ppermute(values, "seq", onward)
    next_values = lax.ppermute(values, "seq", back)
    later_latent, prev_values, next_values = lax.optimization_barrier(
        (latent, prev_values, next_values)
    )
    prev_latent = lax.ppermute(later_latent, "seq", onward)
    next_latent = lax.ppermute(later_latent, "seq", back)

    predicted_maps, outgoing = pl.pallas_call(
        decode_kernel,
        grid=(BLOCKS,),
        in_specs=[
            whole(variables, nodes),
            whole(variables, nodes),
            whole(variables, nodes),
            pl.BlockSpec((1, window, block), lambda i: (i, 0, 0)),
        ],
        out_specs=[
            pl.BlockSpec((1, variables, block), lambda i: (0, 0, i)),
            pl.BlockSpec((block // share, variables, share), lambda i: (i, 0, 0)),
        ],
        out_shape=[
            jax.ShapeDtypeStruct((1, variables, cells), BF16),
            jax.ShapeDtypeStruct((members, variables, share), BF16),
        ],
        scratch_shapes=[pltpu.VMEM((variables, 3 * nodes), BF16)],
        compiler_params=params(32),
        cost_estimate=pl.CostEstimate(
            flops=10**9, bytes_accessed=12 * 10**6, transcendentals=0
        ),
        name="decode_cells",
    )(prev_values, values, next_values, weave)

    incoming = lax.all_to_all(outgoing, "member", split_axis=0, concat_axis=0, tiled=True)
    member_place = lax.axis_index("member")
    truth = lax.dynamic_slice_in_dim(targets, member_place * share, share, 1)
    weight = lax.dynamic_slice_in_dim(area_weight, member_place * share, share, 0)[None, :]
    lanes = 128
    grads, loss = pl.pallas_call(
        functools.partial(score_kernel, members, total_cells),
        grid=(share // lanes,),
        in_specs=[
            pl.BlockSpec((members, variables, lanes), lambda i: (0, 0, i)),
            pl.BlockSpec((variables, lanes), lambda i: (0, i)),
            pl.BlockSpec((1, lanes), lambda i: (0, i)),
        ],
        out_specs=[
            pl.BlockSpec((members, variables, lanes), lambda i: (0, 0, i)),
            pl.BlockSpec((1, lanes), lambda i: (0, i)),
        ],
        out_shape=[
            jax.ShapeDtypeStruct((members, variables, share), BF16),
            jax.ShapeDtypeStruct((1, share), F32),
        ],
        compiler_params=params(32),
        cost_estimate=pl.CostEstimate(
            flops=10**8, bytes_accessed=2 * 10**6, transcendentals=2 * 10**6
        ),
        name="score",
    )(incoming, truth, weight)

    own_grads = lax.all_to_all(grads, "member", split_axis=0, concat_axis=0, tiled=True)
    rows = 128
    partial_grad = pl.pallas_call(
        gradient_kernel,
        grid=(BLOCKS,),
        in_specs=[
            pl.BlockSpec((block // share, variables, share), lambda i: (i, 0, 0)),
            pl.BlockSpec((1, window, block), lambda i: (i, 0, 0)),
            whole(nodes, width),
            whole(nodes, width),
            whole(nodes, width),
            whole(1, share),
        ],
        out_specs=whole(members, rows, width // members),
        out_shape=jax.ShapeDtypeStruct((members, rows, width // members), F32),
        scratch_shapes=[pltpu.VMEM((variables, 3 * nodes), F32)],
        compiler_params=params(40),
        cost_estimate=pl.CostEstimate(
            flops=2 * 10**9, bytes_accessed=14 * 10**6, transcendentals=0
        ),
        name="gradient",
    )(own_grads, weave, prev_latent, latent, next_latent, loss)

    chunk = summed_over(partial_grad, "member")
    piece = summed_over(chunk.reshape(seq_count, rows // seq_count, width // members), "seq")
    chunk = gathered_over(piece, "seq").reshape(rows, width // members)
    total = gathered_over(chunk, "member")
    scoring_penalty = total[0, variables, 0]
    readout_matrix_derivative = (
        total[:, :variables, :].transpose(0, 2, 1).reshape(width, variables)
    )
    return (predicted_maps, scoring_penalty, readout_matrix_derivative)


def solution(mesh):
    placed = (
        P("member", "seq", None),
        P(),
        P(),
        P(),
        P("seq"),
        P(),
        P(None, "seq"),
        P(None, "seq"),
        P(None, "seq"),
        P("seq"),
    )
    return jax.shard_map(
        on_device,
        mesh=mesh,
        in_specs=placed,
        out_specs=(P("member", None, "seq"), P(), P()),
        check_vma=False,
    )
```

time: 700 us -> 192 us (0.27)
  waiting for transfers between devices: 238 us -> 18.7 us
  other arithmetic: 137 us -> 0.18 us
  local copies, waits for them, and re-layouts: 130 us -> 22.1 us
  Pallas kernels: 0 us -> 64.4 us
  matrix products: 55.5 us -> 0 us
  blocking collectives: 88.6 us -> 54.3 us
  between operations: 15.3 us -> 0.85 us
    psum x1 -> x0, waiting for transfers between devices: 170 us -> none  [on_device(): lax.psum((partial_grad, loss_part), ('member', 'seq'))]
    psum x1 -> x0, blocking collectives: 88.6 us -> none  [on_device(): lax.psum((partial_grad, loss_part), ('member', 'seq'))]
    scatter-add x1 -> x0, other arithmetic: 66.9 us -> none  [on_device(): jax.ops.segment_sum(terms.reshape(-1, terms.shape[2]), spread_index, num_...]
    pallas_call x0 -> x6, Pallas kernels: none -> 64.4 us  [the longest x1 27.7 us: on_device(): pl.pallas_call(halo_kernel, grid=(STEPS,), in_specs=[pl.BlockSpec(memory_...]
    all_to_all x0 -> x4, blocking collectives: none -> 54.3 us  [the longest x2 28.3 us: summed_over(): lax.all_to_all(value, axis, split_axis=0, concat_axis=0, tiled=True)]
    gather x1 -> x0, local copies, waits for them, and re-layouts: 43.3 us -> none  [on_device(): picked = table[local_index].astype(jnp.float32)]
    ppermute x6, waiting for transfers between devices: 45.6 us -> 7.38 us  [the longest x1 7.37 us: on_device(): prev_latent = lax.ppermute(later_latent, 'seq', onward)]
    dot_general x6 -> x0, matrix products: 36.5 us -> none  [the longest x2 24.2 us: one_group(): jnp.einsum('hqk,khd->qhd', probs, value_heads, preferred_element_type=jnp...]
  transfers between devices with their start and end apart: 9 -> 8, of which waited for: 9 -> 3; matrix products, arithmetic and copies ran while one was open for 1% -> 5% of each run, Pallas kernels for 0% -> 14%
where the time goes in v1:
time: 192 us; the launch traced here: 190 us
  Pallas kernels  64.4 us (34%)
  blocking collectives  54.3 us (28%)
  starting transfers between devices  29.2 us (15%)
  local copies, waits for them, and re-layouts  22.1 us (12%)
  waiting for transfers between devices  18.7 us (10%)
    all_to_all x2, blocking collectives, summed_over(): lax.all_to_all(value, axis, split_axis=0, concat_axis=0, tiled=True)  28.3 us
    pallas_call x1, Pallas kernels, on_device(): pl.pallas_call(halo_kernel, grid=(STEPS,), in_specs=[pl.BlockSpec(memory_...  27.7 us
    all_to_all x2, blocking collectives, gathered_over(): return lax.all_to_all(copies, axis, split_axis=0, concat_axis=0, tiled=True)  25.9 us
    pallas_call x1, Pallas kernels, on_device(): pl.pallas_call(own_kernel, grid=(STEPS,), in_specs=[whole(nodes, width),...  18.4 us
    unnamed x34, local copies, waits for them, and re-layouts  16.6 us
    ppermute x1, waiting for transfers between devices, on_device(): prev_latent = lax.ppermute(later_latent, 'seq', onward)  7.37 us
    ppermute x1, starting transfers between devices, on_device(): next_state = lax.ppermute(state, 'seq', back)  6.82 us
    all_to_all x1, waiting for transfers between devices, on_device(): lax.all_to_all(outgoing, 'member', split_axis=0, concat_axis=0, tiled=True)  6.28 us
  transfers between devices with their start and end apart: 8, of which 3 were waited for; matrix products, arithmetic and copies ran while one was open for 5% of the time, Pallas kernels for 14%

profile of v1, /device:TPU:2, one launch (start us, length us, event | category | flops | bytes accessed | tf_op | source)
XLA Modules:
  0.0 189.7 jit_solution(12400870693529232387)
XLA Ops:
  0.6 1.7 collective-permute-start
  2.3 6.8 %collective-permute-start.1 = (bf16[512,1024]{1,0:T(8,128)(2,1)}, bf16[512,1024]{1,0:T(8,128)(2,1)}, u32[]{:S(2)}, u32[]{:S(2)}) collective-permute-start(bf16[512,1024]{1,0:T(8,128)(2,1)} %bitcast.25), channel_id=1, source_target_pairs={{1,0},{2,1},{3,2},{4,3},{5,4},{6,5},{7,6},{8,7},{9,8},{10,9},{11,1... | collective-permute-start | bytes 3145736 | tf_op jit(solution)/shard_map/ppermute | solution.py:301
  9.1 4.0 %fusion.5 = (bf16[1024,1024]{1,0:T(8,128)(2,1)}, bf16[1024,1024]{1,0:T(8,128)(2,1)S(1)}) fusion(bf16[1024,3072]{1,0:T(8,128)(2,1)} %wk_ref.3), kind=kLoop, calls=%fused_computation.14 | loop fusion | bytes 8388608 | tf_op jit(solution)/shard_map/slice | solution.py:306
  13.1 2.5 %copy.28 = bf16[1024,1024]{0,1:T(8,128)(2,1)} copy(bf16[1024,1024]{1,0:T(8,128)(2,1)S(1)} %get-tuple-element.28) | data formatting | bytes 4194304
  15.7 2.9 %copy.29 = bf16[1024,1024]{0,1:T(8,128)(2,1)S(1)} copy(bf16[1024,1024]{1,0:T(8,128)(2,1)} %get-tuple-element.27) | data formatting | bytes 4194304
  18.7 2.2 %copy-done.4 = bf16[1024,1024]{0,1:T(8,128)(2,1)S(1)} copy-done((bf16[1024,1024]{0,1:T(8,128)(2,1)S(1)}, bf16[1024,1024]{0,1:T(8,128)(2,1)}, u32[]{:S(2)}) %copy-start.4) | copy-done | bytes 2097176
  22.1 18.4 %own_window.1 = (bf16[1024,512]{1,0:T(8,128)(2,1)S(1)}, f32[1024,512]{1,0:T(8,128)S(1)}, f32[4,8,512]{2,1,0:T(8,128)S(1)}) custom-call(bf16[512,1024]{1,0:T(8,128)(2,1)S(1)} %bitcast.26, f32[1,1024]{1,0:T(1,128)S(1)} %bitcast.29, s32[1,512]{1,0:T(1,128)S(1)} %bitcast.31, bf16[1024,1024]{1,0:T(8,128)(2,1)S(1)} %bitcast.22, bf16[1024,3072]{1,0:T(8,128)(2,1)} %wk_ref.3, ...), custom_call_target="tpu_custom_call" | custom-call | flops 20000000000 | bytes 12000000 | tf_op jit(solution)/shard_map/own_window/pallas_call | solution.py:309
  41.9 27.7 %halo_window.1 = (bf16[512,1024]{1,0:T(8,128)(2,1)S(1)}, bf16[100,512]{1,0:T(8,128)(2,1)S(1)}) custom-call(s32[2]{0:T(128)S(1)} %pad_add_fusion.place_ref, bf16[512,1024]{1,0:T(8,128)(2,1)} %collective-permute-done.prev_ref, bf16[512,1024]{1,0:T(8,128)(2,1)} %collective-permute-done.1.next_ref, bf16[512,1024]{1,0:T(8,128)(2,1)S(1)} %bitcast.27, ...), custom_call_target="tpu_custom_call" | custom-call | flops 30000001024 | bytes 16000000 | tf_op jit(solution)/shard_map/halo_window/pallas_call | solution.py:359
  69.9 5.3 %collective-permute-start.3 = (bf16[100,512]{1,0:T(8,128)(2,1)S(1)}, bf16[100,512]{1,0:T(8,128)(2,1)S(1)}, u32[]{:S(2)}, u32[]{:S(2)}) collective-permute-start(bf16[100,512]{1,0:T(8,128)(2,1)S(1)} %get-tuple-element.19.own_ref), channel_id=1, source_target_pairs={{1,0},{2,1},{3,2},{4,3},{5,4},{6,5},{7,6},{8,7},{9,8},{10,9},{11,1... | collective-permute-start | bytes 307208 | tf_op jit(solution)/shard_map/ppermute | solution.py:409
  75.2 5.7 %weave.1.weave_ref = bf16[4,1152,1024]{2,1,0:T(8,128)(2,1)S(1)} custom-call(s32[3,4096]{1,0:T(4,128)S(1)} %broadcast_subtract_fusion.index_ref, f32[3,4096]{1,0:T(4,128)S(1)} %copy-done.7), custom_call_target="tpu_custom_call" | custom-call | flops 1000000000 | bytes 10000000 | tf_op jit(solution)/shard_map/weave/pallas_call | solution.py:342
  81.0 3.9 %decode_cells.1 = (bf16[1,100,4096]{2,1,0:T(8,128)(2,1)}, bf16[8,100,512]{2,1,0:T(8,128)(2,1)S(1)}) custom-call(bf16[100,512]{1,0:T(8,128)(2,1)S(1)} %collective-permute-done.2.prev_ref, bf16[100,512]{1,0:T(8,128)(2,1)S(1)} %get-tuple-element.19.own_ref, bf16[100,512]{1,0:T(8,128)(2,1)S(1)} %collective-permute-done.3.next_ref, ...), custom_call_target="tpu_custom_call" | custom-call | flops 1000000000 | bytes 12000000 | tf_op jit(solution)/shard_map/decode_cells/pallas_call | solution.py:416
  85.8 4.8 %all-to-all-start = ((bf16[8,100,512]{2,1,0:T(8,128)(2,1)}), bf16[8,100,512]{2,1,0:T(8,128)(2,1)S(1)}, u32[]{:S(2)}, u32[]{:S(2)}) async-start(bf16[8,100,512]{2,1,0:T(8,128)(2,1)} %copy-done.5), calls=%async_computation | async-start | bytes 1703936 | tf_op jit(solution)/shard_map/all_to_all | solution.py:441
  90.7 5.3 %collective-permute-start.5 = (bf16[512,1024]{1,0:T(8,128)(2,1)S(1)}, bf16[512,1024]{1,0:T(8,128)(2,1)}, u32[]{:S(2)}, u32[]{:S(2)}) collective-permute-start(bf16[512,1024]{1,0:T(8,128)(2,1)S(1)} %get-tuple-element.25.own_ref), channel_id=1, source_target_pairs={{1,0},{2,1},{3,2},{4,3},{5,4},{6,5},{7,6},{8,7},{9,8},{10,9},{11,1... | collective-permute-start | bytes 3145736 | tf_op jit(solution)/shard_map/ppermute | solution.py:414
  96.8 6.3 %all-to-all-done.maps_ref = bf16[8,100,512]{2,1,0:T(8,128)(2,1)S(1)} async-done(((bf16[8,100,512]{2,1,0:T(8,128)(2,1)}), bf16[8,100,512]{2,1,0:T(8,128)(2,1)S(1)}, u32[]{:S(2)}, u32[]{:S(2)}) %all-to-all-start) | async-done | bytes 819232 | tf_op jit(solution)/shard_map/all_to_all | solution.py:441
  103.1 3.0 %score.1 = (bf16[8,100,512]{2,1,0:T(8,128)(2,1)S(1)}, f32[1,512]{1,0:T(1,128)S(1)}) custom-call(bf16[8,100,512]{2,1,0:T(8,128)(2,1)S(1)} %all-to-all-done.maps_ref, bf16[100,512]{1,0:T(8,128)(2,1)S(1)} %constant_dynamic-slice_fusion.truth_ref, f32[1,512]{1,0:T(1,128)S(1)} %bitcast.23), custom_call_target="tpu_custom_call" | custom-call | flops 100000000 | bytes 2000000 | tf_op jit(solution)/shard_map/score/pallas_call | solution.py:446
  107.0 4.9 %all-to-all-start.1 = ((bf16[8,100,512]{2,1,0:T(8,128)(2,1)}), bf16[8,100,512]{2,1,0:T(8,128)(2,1)S(1)}, u32[]{:S(2)}, u32[]{:S(2)}) async-start(bf16[8,100,512]{2,1,0:T(8,128)(2,1)} %copy-done.6), calls=%async_computation.1 | async-start | bytes 1703936 | tf_op jit(solution)/shard_map/all_to_all | solution.py:469
  111.9 7.4 %collective-permute-done.4.prev_ref = bf16[512,1024]{1,0:T(8,128)(2,1)} collective-permute-done((bf16[512,1024]{1,0:T(8,128)(2,1)S(1)}, bf16[512,1024]{1,0:T(8,128)(2,1)}, u32[]{:S(2)}, u32[]{:S(2)}) %collective-permute-start.4) | collective-permute-done | bytes 1048608 | tf_op jit(solution)/shard_map/ppermute | solution.py:413
  119.3 5.1 %all-to-all-done.1.grad_ref = bf16[8,100,512]{2,1,0:T(8,128)(2,1)S(1)} async-done(((bf16[8,100,512]{2,1,0:T(8,128)(2,1)}), bf16[8,100,512]{2,1,0:T(8,128)(2,1)S(1)}, u32[]{:S(2)}, u32[]{:S(2)}) %all-to-all-start.1) | async-done | bytes 819232 | tf_op jit(solution)/shard_map/all_to_all | solution.py:469
  124.4 3.7 %copy-done.2 = bf16[4,1152,1024]{2,1,0:T(8,128)(2,1)S(1)} copy-done((bf16[4,1152,1024]{2,1,0:T(8,128)(2,1)S(1)}, bf16[4,1152,1024]{2,1,0:T(8,128)(2,1)}, u32[]{:S(2)}) %copy-start.2) | copy-done | bytes 9437208
  128.0 5.7 %gradient.1 = f32[8,128,128]{2,1,0:T(8,128)S(1)} custom-call(bf16[8,100,512]{2,1,0:T(8,128)(2,1)S(1)} %all-to-all-done.1.grad_ref, bf16[4,1152,1024]{2,1,0:T(8,128)(2,1)S(1)} %copy-done.2, bf16[512,1024]{1,0:T(8,128)(2,1)} %collective-permute-done.4.prev_ref, bf16[512,1024]{1,0:T(8,128)(2,1)S(1)} %get-tuple-element.25.own_ref, ...), custom_call_target="tpu_custom_call" | custom-call | flops 2000000000 | bytes 14000000 | tf_op jit(solution)/shard_map/gradient/pallas_call | solution.py:471
  133.8 12.8 %all_to_all.30 = f32[8,128,128]{2,1,0:T(8,128)S(1)} all-to-all(f32[8,128,128]{2,1,0:T(8,128)S(1)} %gradient.1), channel_id=1, replica_groups=mesh['member'=8,'seq'=32] {'member'}, dimensions={0} | all-to-all | bytes 1048576 | tf_op jit(solution)/shard_map/all_to_all | solution.py:269
  146.6 15.5 %all_to_all.31 = f32[32,4,128]{2,1,0:T(4,128)S(1)} all-to-all(f32[32,4,128]{2,1,0:T(4,128)S(1)} %bitcast.37), channel_id=1, replica_groups=mesh['member'=8,'seq'=32] {'seq'}, dimensions={0} | all-to-all | bytes 131072 | tf_op jit(solution)/shard_map/all_to_all | solution.py:269
  162.2 13.1 %all_to_all.32 = f32[32,4,128]{2,1,0:T(4,128)S(1)} all-to-all(f32[32,4,128]{2,1,0:T(4,128)S(1)} %broadcast_in_dim.26), channel_id=1, replica_groups=mesh['member'=8,'seq'=32] {'seq'}, dimensions={0} | all-to-all | bytes 131072 | tf_op jit(solution)/shard_map/all_to_all | solution.py:274
  175.4 12.8 %all_to_all.33 = f32[8,128,128]{2,1,0:T(8,128)S(1)} all-to-all(f32[8,128,128]{2,1,0:T(8,128)S(1)} %broadcast_in_dim.28), channel_id=1, replica_groups=mesh['member'=8,'seq'=32] {'member'}, dimensions={0} | all-to-all | bytes 1048576 | tf_op jit(solution)/shard_map/all_to_all | solution.py:274
  (49 shorter events, 7.2 us)
Async XLA Ops:
  0.6 96.1 %copy-start = (bf16[100,4096]{1,0:T(8,128)(2,1)S(1)}, bf16[100,4096]{1,0:T(8,128)(2,1)}, u32[]{:S(2)}) copy-start(bf16[100,4096]{1,0:T(8,128)(2,1)} %param.18) | copy-start | bytes 2457604
  0.6 41.2 %collective-permute-start = (bf16[512,1024]{1,0:T(8,128)(2,1)}, bf16[512,1024]{1,0:T(8,128)(2,1)}, u32[]{:S(2)}, u32[]{:S(2)}) collective-permute-start(bf16[512,1024]{1,0:T(8,128)(2,1)} %bitcast.24), channel_id=1, source_target_pairs={{0,1},{1,2},{2,3},{3,4},{4,5},{5,6},{6,7},{7,8},{8,9},{9,10},{10,1... | collective-permute-start | bytes 3145736 | tf_op jit(solution)/shard_map/ppermute | solution.py:300
  2.3 39.6 %collective-permute-start.1 = (bf16[512,1024]{1,0:T(8,128)(2,1)}, bf16[512,1024]{1,0:T(8,128)(2,1)}, u32[]{:S(2)}, u32[]{:S(2)}) collective-permute-start(bf16[512,1024]{1,0:T(8,128)(2,1)} %bitcast.25), channel_id=1, source_target_pairs={{1,0},{2,1},{3,2},{4,3},{5,4},{6,5},{7,6},{8,7},{9,8},{10,9},{11,1... | collective-permute-start | bytes 3145736 | tf_op jit(solution)/shard_map/ppermute | solution.py:301
  15.7 3.0 %copy-start.11 = (f32[1024]{0:T(1024)S(1)}, f32[1024]{0:T(1024)}, u32[]{:S(2)}) copy-start(f32[1024]{0:T(1024)} %param.11) | copy-start | bytes 12292
  15.7 3.0 %copy-start.12 = (s32[512]{0:T(512)S(1)}, s32[512]{0:T(512)}, u32[]{:S(2)}) copy-start(s32[512]{0:T(512)} %param.14) | copy-start | bytes 6148
  18.6 22.0 %copy-start.3 = (bf16[1024,1024]{0,1:T(8,128)(2,1)}, bf16[1024,1024]{0,1:T(8,128)(2,1)S(1)}, u32[]{:S(2)}) copy-start(bf16[1024,1024]{0,1:T(8,128)(2,1)S(1)} %copy.29) | copy-start | bytes 6291460
  18.7 2.2 %copy-start.4 = (bf16[1024,1024]{0,1:T(8,128)(2,1)S(1)}, bf16[1024,1024]{0,1:T(8,128)(2,1)}, u32[]{:S(2)}) copy-start(bf16[1024,1024]{0,1:T(8,128)(2,1)} %copy.28) | copy-start | bytes 6291460
  20.9 1.2 copy-start.8
  22.1 19.7 %copy-start.9 = (bf16[1,512,1024]{2,1,0:T(8,128)(2,1)S(1)}, bf16[1,512,1024]{2,1,0:T(8,128)(2,1)}, u32[]{:S(2)}) copy-start(bf16[1,512,1024]{2,1,0:T(8,128)(2,1)} %param.10) | copy-start | bytes 3145732
  22.1 19.7 %copy-start.10 = (bf16[1024,100]{0,1:T(8,128)(2,1)S(1)}, bf16[1024,100]{0,1:T(8,128)(2,1)}, u32[]{:S(2)}) copy-start(bf16[1024,100]{0,1:T(8,128)(2,1)} %param.15) | copy-start | bytes 614404
  40.6 1.3 copy-start.13
  41.9 33.3 %copy-start.14 = (s32[3,4096]{1,0:T(4,128)S(1)}, s32[3,4096]{1,0:T(4,128)}, u32[]{:S(2)}) copy-start(s32[3,4096]{1,0:T(4,128)} %param.16) | copy-start | bytes 147460
  41.9 33.3 %copy-start.7 = (f32[3,4096]{1,0:T(4,128)S(1)}, f32[3,4096]{1,0:T(4,128)}, u32[]{:S(2)}) copy-start(f32[3,4096]{1,0:T(4,128)} %coeff_ref.1) | copy-start | bytes 147460
  69.6 11.3 %collective-permute-start.2 = (bf16[100,512]{1,0:T(8,128)(2,1)S(1)}, bf16[100,512]{1,0:T(8,128)(2,1)S(1)}, u32[]{:S(2)}, u32[]{:S(2)}) collective-permute-start(bf16[100,512]{1,0:T(8,128)(2,1)S(1)} %get-tuple-element.19.own_ref), channel_id=1, source_target_pairs={{0,1},{1,2},{2,3},{3,4},{4,5},{5,6},{6,7},{7,8},{8,9},{9,10},{10,1... | collective-permute-start | bytes 307208 | tf_op jit(solution)/shard_map/ppermute | solution.py:408
  69.9 11.1 %collective-permute-start.3 = (bf16[100,512]{1,0:T(8,128)(2,1)S(1)}, bf16[100,512]{1,0:T(8,128)(2,1)S(1)}, u32[]{:S(2)}, u32[]{:S(2)}) collective-permute-start(bf16[100,512]{1,0:T(8,128)(2,1)S(1)} %get-tuple-element.19.own_ref), channel_id=1, source_target_pairs={{1,0},{2,1},{3,2},{4,3},{5,4},{6,5},{7,6},{8,7},{9,8},{10,9},{11,1... | collective-permute-start | bytes 307208 | tf_op jit(solution)/shard_map/ppermute | solution.py:409
  80.9 4.0 %copy-start.1 = (bf16[4,1152,1024]{2,1,0:T(8,128)(2,1)}, bf16[4,1152,1024]{2,1,0:T(8,128)(2,1)S(1)}, u32[]{:S(2)}) copy-start(bf16[4,1152,1024]{2,1,0:T(8,128)(2,1)S(1)} %weave.1.weave_ref) | copy-start | bytes 28311556
  84.9 0.9 copy-start.5
  85.8 17.2 %all-to-all-start = ((bf16[8,100,512]{2,1,0:T(8,128)(2,1)}), bf16[8,100,512]{2,1,0:T(8,128)(2,1)S(1)}, u32[]{:S(2)}, u32[]{:S(2)}) async-start(bf16[8,100,512]{2,1,0:T(8,128)(2,1)} %copy-done.5), calls=%async_computation | async-start | bytes 1703936 | tf_op jit(solution)/shard_map/all_to_all | solution.py:441
  90.7 28.6 %collective-permute-start.4 = (bf16[512,1024]{1,0:T(8,128)(2,1)S(1)}, bf16[512,1024]{1,0:T(8,128)(2,1)}, u32[]{:S(2)}, u32[]{:S(2)}) collective-permute-start(bf16[512,1024]{1,0:T(8,128)(2,1)S(1)} %get-tuple-element.25.own_ref), channel_id=1, source_target_pairs={{0,1},{1,2},{2,3},{3,4},{4,5},{5,6},{6,7},{7,8},{8,9},{9,10},{10,1... | collective-permute-start | bytes 3145736 | tf_op jit(solution)/shard_map/ppermute | solution.py:413
  90.7 28.6 %collective-permute-start.5 = (bf16[512,1024]{1,0:T(8,128)(2,1)S(1)}, bf16[512,1024]{1,0:T(8,128)(2,1)}, u32[]{:S(2)}, u32[]{:S(2)}) collective-permute-start(bf16[512,1024]{1,0:T(8,128)(2,1)S(1)} %get-tuple-element.25.own_ref), channel_id=1, source_target_pairs={{1,0},{2,1},{3,2},{4,3},{5,4},{6,5},{7,6},{8,7},{9,8},{10,9},{11,1... | collective-permute-start | bytes 3145736 | tf_op jit(solution)/shard_map/ppermute | solution.py:414
  106.1 0.9 copy-start.6
  107.0 17.3 %all-to-all-start.1 = ((bf16[8,100,512]{2,1,0:T(8,128)(2,1)}), bf16[8,100,512]{2,1,0:T(8,128)(2,1)S(1)}, u32[]{:S(2)}, u32[]{:S(2)}) async-start(bf16[8,100,512]{2,1,0:T(8,128)(2,1)} %copy-done.6), calls=%async_computation.1 | async-start | bytes 1703936 | tf_op jit(solution)/shard_map/all_to_all | solution.py:469
  124.4 3.7 %copy-start.2 = (bf16[4,1152,1024]{2,1,0:T(8,128)(2,1)S(1)}, bf16[4,1152,1024]{2,1,0:T(8,128)(2,1)}, u32[]{:S(2)}) copy-start(bf16[4,1152,1024]{2,1,0:T(8,128)(2,1)} %copy-done.1) | copy-start | bytes 28311556
